TPU v7x, 32 devices: a whole 2x2x4 slice. The times are simulated.
32 devices in a mesh: seq: 8 (over y, x, core), blk: 4 (over z).
Axes of the slice: x: 2, y: 2, z: 4, core: 2. Of those that a mesh axis runs over, the one named last changes fastest.
Arguments:
- stem_tokens: bfloat16 [128, 24, 128, 128], P('blk', 'seq'), may hold values from -6 to 6
- view_code: int32 [128, 24], P('blk', 'seq'), may hold values from 1 to 7
- cotangent: bfloat16 [2048, 24, 128], P('blk', 'seq'), may hold values from -6 to 6
- stem_queries: bfloat16 [16, 128], replicated, may hold values from -8 to 8
- w_stem_kv: bfloat16 [128, 256], replicated, may hold values from -0.5 to 0.5
- w_stem_out: bfloat16 [128, 128], replicated, may hold values from -1.5 to 1.5
- gain_one: float32 [128], replicated, may hold values from 0.1 to 1.9
- w_qkv: bfloat16 [128, 384], replicated, may hold values from -0.5 to 0.5
- w_attn_out: bfloat16 [128, 128], replicated, may hold values from -2 to 2
- gain_two: float32 [128], replicated, may hold values from 0.1 to 1.9
- w_up: bfloat16 [128, 512], replicated, may hold values from -0.5 to 0.5
- w_down: bfloat16 [512, 128], replicated, may hold values from -0.25 to 0.25
Outputs:
- block_out: bfloat16 [2048, 24, 128], P('blk', 'seq')
- grad_input: float32 [128, 24, 128, 128], P('blk', 'seq')
- grad_stem_queries: float32 [16, 128], P('blk')
- grad_w_stem_kv: float32 [128, 256], P('blk')
- grad_w_stem_out: float32 [128, 128], P('blk')
- grad_gain_one: float32 [128], P('blk')
- grad_w_qkv: float32 [128, 384], P('blk')
- grad_w_attn_out: float32 [128, 128], P('blk')
- grad_gain_two: float32 [128], P('blk')
- grad_w_up: float32 [128, 512], P('blk')
- grad_w_down: float32 [512, 128], P('blk')
Inputs may be any that keep to these rules, and one draw needn't show every extreme that they name: `view_code`: bit v (v = 0, 1, 2) of a code is 1 where view v is present at that timestep; every timestep has a view.
All inputs are finite; a program needn't handle non-finite values.
Results may differ from a plain program's by a relative error of at most 0.02.
Values may be sent and summed in bfloat16 or wider, within the bound.
A program may use at most 128 MiB of HBM per device.

v0:
```python
import math

import jax
import jax.numpy as jnp
from jax import lax
from jax.sharding import PartitionSpec as P

HEADS = 8
IMG_TOK = 32


EPSILON = 1e-05
NEGATIVE_FILL = -1e30


def rounded(values_in):
    return lax.optimization_barrier(values_in.astype(jnp.bfloat16)).astype(jnp.float32)


def norm_parts(values_in, gain_vector):
    center = values_in - jnp.mean(values_in, axis=-1, keepdims=True)
    inverse_rows = lax.rsqrt(jnp.mean(center * center, axis=-1, keepdims=True) + EPSILON)
    unit_rows = center * inverse_rows
    return (unit_rows * gain_vector, unit_rows, inverse_rows)


def norm_backward(grad_out, unit_rows, inverse_rows, gain_vector):
    grad_unit = grad_out * gain_vector
    grad_gain = jnp.sum(grad_out * unit_rows, axis=(0, 1))
    centered = grad_unit - jnp.mean(grad_unit, axis=-1, keepdims=True)
    grad_in = inverse_rows * (
        centered - unit_rows * jnp.mean(grad_unit * unit_rows, axis=-1, keepdims=True)
    )
    return (grad_in, grad_gain)


def visible_keys(view_code, key_count):
    positions = jnp.arange(key_count, dtype=jnp.int32)
    view_slot = jnp.minimum(positions // IMG_TOK, 2)
    present = jnp.right_shift(view_code[:, :, None], view_slot[None, None, :]) % 2
    return (present == 1) | (positions[None, None, :] >= 3 * IMG_TOK)


def heads_first(rows_in):
    row_count, seq_count, model_width = rows_in.shape
    return rows_in.reshape(row_count, seq_count, HEADS, model_width // HEADS).transpose(1, 2, 0, 3)


def rows_first(heads_in):
    seq_count, head_count, row_count, head_size = heads_in.shape
    return heads_in.transpose(2, 0, 1, 3).reshape(row_count, seq_count, head_count * head_size)


def attend_piece(
    carry, key_rows, value_rows, start, query_heads, query_steps, query_count, score_scale
):
    piece_rows = key_rows.shape[0]
    key_steps = (start + jnp.arange(piece_rows, dtype=jnp.int32)) // query_count
    allowed = key_steps[None, :] <= query_steps[:, None]
    key_heads = heads_first(key_rows)
    value_heads = heads_first(value_rows)

    def attend_per_sequence(operands):
        top_old, total_old, accum_old, query_seq, key_seq, value_seq = operands
        scores = (
            jnp.einsum("hte,hre->htr", query_seq, key_seq, preferred_element_type=jnp.float32)
            * score_scale
        )
        scores = jnp.where(allowed[None], scores, NEGATIVE_FILL)
        top_new = jnp.maximum(top_old, jnp.max(scores, axis=-1))
        expanded = jnp.where(allowed[None], jnp.exp(scores - top_new[..., None]), 0.0)
        rescale = jnp.exp(top_old - top_new)
        total_new = total_old * rescale + jnp.sum(expanded, axis=-1)
        weighted = jnp.einsum(
            "htr,hre->hte",
            expanded.astype(jnp.bfloat16),
            value_seq,
            preferred_element_type=jnp.float32,
        )
        return (top_new, total_new, accum_old * rescale[..., None] + weighted)

    return lax.map(
        attend_per_sequence, (carry[0], carry[1], carry[2], query_heads, key_heads, value_heads)
    )


def guarded_piece(
    carry, key_rows, value_rows, start, query_heads, query_steps, query_count, score_scale
):
    beyond = start // query_count > query_steps[-1]

    def guarded_work(carry_in):
        return attend_piece(
            carry_in,
            key_rows,
            value_rows,
            start,
            query_heads,
            query_steps,
            query_count,
            score_scale,
        )

    def guarded_keep(carry_in):
        return carry_in

    return lax.cond(beyond, guarded_keep, guarded_work, carry)


def fold_piece(carry, key_rows, value_rows, query_heads, query_steps, query_count, score_scale):
    piece_rows = key_rows.shape[0]
    block_rows = 512

    def loop_body(block_index, carry_in):
        offset = block_index * block_rows
        key_block = lax.dynamic_slice_in_dim(key_rows, offset, block_rows, 0)
        value_block = lax.dynamic_slice_in_dim(value_rows, offset, block_rows, 0)
        return guarded_piece(
            carry_in,
            key_block,
            value_block,
            offset,
            query_heads,
            query_steps,
            query_count,
            score_scale,
        )

    return lax.fori_loop(0, piece_rows // block_rows, loop_body, carry)


def per_device(
    stem_tokens,
    view_code,
    cotangent,
    stem_queries,
    w_stem_kv,
    w_stem_out,
    gain_one,
    w_qkv,
    w_attn_out,
    gain_two,
    w_up,
    w_down,
):
    step_count, seq_count, key_count, model_width = stem_tokens.shape
    query_count = stem_queries.shape[0]
    head_size = model_width // HEADS
    score_scale = 1.0 / math.sqrt(head_size)
    token_rows = step_count * query_count
    key_value = jnp.einsum(
        "tskd,de->tske", stem_tokens, w_stem_kv, preferred_element_type=jnp.float32
    ).astype(jnp.bfloat16)
    stem_keys = key_value[..., :model_width].reshape(
        step_count, seq_count, key_count, HEADS, head_size
    )
    stem_values = key_value[..., model_width:].reshape(
        step_count, seq_count, key_count, HEADS, head_size
    )
    stem_query_heads = stem_queries.reshape(query_count, HEADS, head_size)
    stem_scores = (
        jnp.einsum(
            "nhe,tskhe->tshnk", stem_query_heads, stem_keys, preferred_element_type=jnp.float32
        )
        * score_scale
    )
    stem_visible = visible_keys(view_code, key_count)[:, :, None, None, :]
    stem_scores = jnp.where(stem_visible, stem_scores, NEGATIVE_FILL)
    stem_probs = jax.nn.softmax(stem_scores, axis=-1)
    stem_probs_low = stem_probs.astype(jnp.bfloat16)
    stem_mixed = jnp.einsum(
        "tshnk,tskhe->tsnhe", stem_probs_low, stem_values, preferred_element_type=jnp.float32
    )
    stem_mixed_low = stem_mixed.astype(jnp.bfloat16).reshape(
        step_count, seq_count, query_count, model_width
    )
    stem_output = jnp.einsum(
        "tsnd,de->tsne", stem_mixed_low, w_stem_out, preferred_element_type=jnp.float32
    )
    residual = stem_output.transpose(0, 2, 1, 3).reshape(token_rows, seq_count, model_width)
    normed_one, unit_one, inverse_one = norm_parts(residual, gain_one)
    normed_one_low = normed_one.astype(jnp.bfloat16)
    projected = jnp.einsum(
        "tsd,de->tse", normed_one_low, w_qkv, preferred_element_type=jnp.float32
    ).astype(jnp.bfloat16)
    query_part = projected[..., :model_width]
    key_part = projected[..., model_width : 2 * model_width]
    value_part = projected[..., 2 * model_width :]
    query_heads = heads_first(query_part)
    query_steps = (
        lax.axis_index("blk") * token_rows + jnp.arange(token_rows, dtype=jnp.int32)
    ) // query_count
    initial = (
        jnp.full((seq_count, HEADS, token_rows), NEGATIVE_FILL, jnp.float32),
        jnp.zeros((seq_count, HEADS, token_rows), jnp.float32),
        jnp.zeros((seq_count, HEADS, token_rows, head_size), jnp.float32),
    )
    folded = fold_piece(
        initial,
        lax.all_gather(key_part, "blk", axis=0, tiled=True),
        lax.all_gather(value_part, "blk", axis=0, tiled=True),
        query_heads,
        query_steps,
        query_count,
        score_scale,
    )
    top_final, total_final, accum_final = folded
    attended = accum_final / total_final[..., None]
    log_total = top_final + jnp.log(total_final)
    attended_low = rows_first(attended).astype(jnp.bfloat16)
    after_attn = residual + jnp.einsum(
        "tsd,de->tse", attended_low, w_attn_out, preferred_element_type=jnp.float32
    )
    normed_two, unit_two, inverse_two = norm_parts(after_attn, gain_two)
    normed_two_low = normed_two.astype(jnp.bfloat16)
    hidden_pre = jnp.einsum("tsd,df->tsf", normed_two_low, w_up, preferred_element_type=jnp.float32)
    hidden_low = jax.nn.gelu(hidden_pre, approximate=False).astype(jnp.bfloat16)
    block_full = after_attn + jnp.einsum(
        "tsf,fd->tsd", hidden_low, w_down, preferred_element_type=jnp.float32
    )
    grad_output = cotangent.astype(jnp.float32)
    grad_down = jnp.einsum("tsf,tsd->fd", hidden_low, cotangent, preferred_element_type=jnp.float32)
    grad_hidden = jnp.einsum("tsd,fd->tsf", cotangent, w_down, preferred_element_type=jnp.float32)

    def gelu_exact(pre_values):
        return jax.nn.gelu(pre_values, approximate=False)

    gelu_pull = jax.vjp(gelu_exact, hidden_pre)[1]
    grad_pre_low = gelu_pull(grad_hidden)[0].astype(jnp.bfloat16)
    grad_up = jnp.einsum(
        "tsd,tsf->df", normed_two_low, grad_pre_low, preferred_element_type=jnp.float32
    )
    grad_normed_two = rounded(
        jnp.einsum("tsf,df->tsd", grad_pre_low, w_up, preferred_element_type=jnp.float32)
    )
    grad_after, grad_gain_two = norm_backward(grad_normed_two, unit_two, inverse_two, gain_two)
    grad_after = grad_after + grad_output
    grad_after_low = grad_after.astype(jnp.bfloat16)
    grad_attn_out = jnp.einsum(
        "tsd,tse->de", attended_low, grad_after_low, preferred_element_type=jnp.float32
    )
    grad_attended = jnp.einsum(
        "tse,de->tsd", grad_after_low, w_attn_out, preferred_element_type=jnp.float32
    ).astype(jnp.bfloat16)
    grad_att_heads = heads_first(grad_attended)
    row_dot = jnp.sum(grad_att_heads.astype(jnp.float32) * attended, axis=-1)
    whole_keys, whole_values = (
        lax.all_gather(key_part, "blk", axis=0, tiled=True),
        lax.all_gather(value_part, "blk", axis=0, tiled=True),
    )
    whole_rows = whole_keys.shape[0]
    key_block = min(512, whole_rows)
    block_total = whole_rows // key_block

    def backward_block(grad_query, block_index):
        start = block_index * key_block
        key_heads = heads_first(lax.dynamic_slice_in_dim(whole_keys, start, key_block, 0))
        value_heads = heads_first(lax.dynamic_slice_in_dim(whole_values, start, key_block, 0))
        key_steps = (start + jnp.arange(key_block, dtype=jnp.int32)) // query_count
        allowed = key_steps[None, :] <= query_steps[:, None]

        def backward_per_sequence(operands):
            query_seq, key_seq, value_seq, grad_att_seq, log_seq, dot_seq, grad_query_seq = operands
            scores = (
                jnp.einsum("hte,hre->htr", query_seq, key_seq, preferred_element_type=jnp.float32)
                * score_scale
            )
            attn_probs = jnp.where(allowed[None], jnp.exp(scores - log_seq[..., None]), 0.0)
            grad_probs = jnp.einsum(
                "hte,hre->htr", grad_att_seq, value_seq, preferred_element_type=jnp.float32
            )
            grad_scores = (attn_probs * (grad_probs - dot_seq[..., None])).astype(jnp.bfloat16)
            grad_query_new = (
                grad_query_seq
                + jnp.einsum(
                    "htr,hre->hte", grad_scores, key_seq, preferred_element_type=jnp.float32
                )
                * score_scale
            )
            grad_key_seq = (
                jnp.einsum(
                    "htr,hte->hre", grad_scores, query_seq, preferred_element_type=jnp.float32
                )
                * score_scale
            )
            grad_value_seq = jnp.einsum(
                "htr,hte->hre",
                attn_probs.astype(jnp.bfloat16),
                grad_att_seq,
                preferred_element_type=jnp.float32,
            )
            return (grad_query_new, grad_key_seq, grad_value_seq)

        def backward_work(grad_query_in):
            grad_query_new, grad_key_heads, grad_value_heads = lax.map(
                backward_per_sequence,
                (
                    query_heads,
                    key_heads,
                    value_heads,
                    grad_att_heads,
                    log_total,
                    row_dot,
                    grad_query_in,
                ),
            )
            return (
                grad_query_new,
                jnp.concatenate(
                    [rows_first(grad_key_heads), rows_first(grad_value_heads)], axis=-1
                ),
            )

        def backward_keep(grad_query_in):
            return (grad_query_in, jnp.zeros((key_block, seq_count, 2 * model_width), jnp.float32))

        return lax.cond(key_steps[0] > query_steps[-1], backward_keep, backward_work, grad_query)

    grad_query_init = jnp.zeros((seq_count, HEADS, token_rows, head_size), jnp.float32)
    grad_query, term_blocks = lax.scan(
        backward_block, grad_query_init, jnp.arange(block_total, dtype=jnp.int32)
    )
    term_all = term_blocks.reshape(whole_rows, seq_count, 2 * model_width)
    grad_key_value = lax.psum_scatter(
        term_all.astype(jnp.bfloat16), "blk", scatter_dimension=0, tiled=True
    ).astype(jnp.float32)
    grad_projected = jnp.concatenate([rows_first(grad_query), grad_key_value], axis=-1).astype(
        jnp.bfloat16
    )
    grad_qkv = jnp.einsum(
        "tsd,tse->de", normed_one_low, grad_projected, preferred_element_type=jnp.float32
    )
    grad_normed_one = rounded(
        jnp.einsum("tse,de->tsd", grad_projected, w_qkv, preferred_element_type=jnp.float32)
    )
    grad_residual, grad_gain_one = norm_backward(grad_normed_one, unit_one, inverse_one, gain_one)
    grad_residual = grad_residual + grad_after
    grad_stem_output = (
        grad_residual.reshape(step_count, query_count, seq_count, model_width)
        .transpose(0, 2, 1, 3)
        .astype(jnp.bfloat16)
    )
    grad_stem_out = jnp.einsum(
        "tsnd,tsne->de", stem_mixed_low, grad_stem_output, preferred_element_type=jnp.float32
    )
    grad_mixed = jnp.einsum(
        "tsne,de->tsnd", grad_stem_output, w_stem_out, preferred_element_type=jnp.float32
    ).astype(jnp.bfloat16)
    grad_mixed_heads = grad_mixed.reshape(step_count, seq_count, query_count, HEADS, head_size)
    stem_dot = jnp.transpose(
        jnp.sum(grad_mixed_heads.astype(jnp.float32) * stem_mixed, axis=-1), (0, 1, 3, 2)
    )
    grad_stem_probs = jnp.einsum(
        "tsnhe,tskhe->tshnk", grad_mixed_heads, stem_values, preferred_element_type=jnp.float32
    )
    grad_stem_scores = (stem_probs * (grad_stem_probs - stem_dot[..., None])).astype(jnp.bfloat16)
    grad_queries = (
        jnp.einsum(
            "tshnk,tskhe->nhe", grad_stem_scores, stem_keys, preferred_element_type=jnp.float32
        ).reshape(query_count, model_width)
        * score_scale
    )
    grad_stem_keys = (
        jnp.einsum(
            "tshnk,nhe->tskhe",
            grad_stem_scores,
            stem_query_heads,
            preferred_element_type=jnp.float32,
        )
        * score_scale
    )
    grad_stem_values = jnp.einsum(
        "tshnk,tsnhe->tskhe", stem_probs_low, grad_mixed_heads, preferred_element_type=jnp.float32
    )
    stem_shape = (step_count, seq_count, key_count, model_width)
    grad_kv_stem = jnp.concatenate(
        [grad_stem_keys.reshape(stem_shape), grad_stem_values.reshape(stem_shape)], axis=-1
    ).astype(jnp.bfloat16)
    grad_stem_kv = jnp.einsum(
        "tskd,tske->de", stem_tokens, grad_kv_stem, preferred_element_type=jnp.float32
    )
    grad_input = jnp.einsum(
        "tske,de->tskd", grad_kv_stem, w_stem_kv, preferred_element_type=jnp.float32
    )
    local_grads = (
        grad_queries,
        grad_stem_kv,
        grad_stem_out,
        grad_gain_one,
        grad_qkv,
        grad_attn_out,
        grad_gain_two,
        grad_up,
        grad_down,
    )
    shares = (
        lax.psum_scatter(
            local_grads[0].astype(jnp.bfloat16), "blk", scatter_dimension=0, tiled=True
        ).astype(jnp.float32),
        lax.psum_scatter(
            local_grads[1].astype(jnp.bfloat16), "blk", scatter_dimension=0, tiled=True
        ).astype(jnp.float32),
        lax.psum_scatter(
            local_grads[2].astype(jnp.bfloat16), "blk", scatter_dimension=0, tiled=True
        ).astype(jnp.float32),
        lax.psum_scatter(
            local_grads[3].astype(jnp.bfloat16), "blk", scatter_dimension=0, tiled=True
        ).astype(jnp.float32),
        lax.psum_scatter(
            local_grads[4].astype(jnp.bfloat16), "blk", scatter_dimension=0, tiled=True
        ).astype(jnp.float32),
        lax.psum_scatter(
            local_grads[5].astype(jnp.bfloat16), "blk", scatter_dimension=0, tiled=True
        ).astype(jnp.float32),
        lax.psum_scatter(
            local_grads[6].astype(jnp.bfloat16), "blk", scatter_dimension=0, tiled=True
        ).astype(jnp.float32),
        lax.psum_scatter(
            local_grads[7].astype(jnp.bfloat16), "blk", scatter_dimension=0, tiled=True
        ).astype(jnp.float32),
        lax.psum_scatter(
            local_grads[8].astype(jnp.bfloat16), "blk", scatter_dimension=0, tiled=True
        ).astype(jnp.float32),
    )
    totals = lax.psum(
        (
            shares[0],
            shares[1],
            shares[2],
            shares[3],
            shares[4],
            shares[5],
            shares[6],
            shares[7],
            shares[8],
        ),
        "seq",
    )
    return (
        block_full.astype(jnp.bfloat16),
        grad_input,
        totals[0],
        totals[1],
        totals[2],
        totals[3],
        totals[4],
        totals[5],
        totals[6],
        totals[7],
        totals[8],
    )


def solution(mesh):
    return jax.shard_map(
        per_device,
        mesh=mesh,
        in_specs=(
            P("blk", "seq", None, None),
            P("blk", "seq"),
            P("blk", "seq", None),
            P(),
            P(),
            P(),
            P(),
            P(),
            P(),
            P(),
            P(),
            P(),
        ),
        out_specs=(
            P("blk", "seq", None),
            P("blk", "seq", None, None),
            P("blk", None),
            P("blk", None),
            P("blk", None),
            P("blk"),
            P("blk", None),
            P("blk", None),
            P("blk"),
            P("blk", None),
            P("blk", None),
        ),
        check_vma=False,
    )
```

profile of v0, /device:TPU:0, one launch (start us, length us, event | category | flops | bytes accessed | tf_op | source)
XLA Modules:
  0.0 843.3 jit_solution(5708673587891577370)
XLA Ops:
  11.7 4.6 fusion.202
  16.3 4.7 copy.123
  21.0 4.6 copy.125
  28.7 130.4 %fusion.204 = (f32[32,3,8,16]{3,1,0,2:T(4,128)S(1)}, f32[32,3,8,16,128]{4,3,1,0,2:T(8,128)S(1)}) fusion(f32[8,32,3,128,16]{3,4,2,1,0:T(8,128)S(1)} %fusion.95, pred[32,3,128]{2,1,0:T(4,128)(4,1)S(1)} %fusion.188), kind=kOutput, calls=%fused_computation.274 | output fusion | flops 9437311 | bytes 12644352 | tf_op jit(solution)/shard_map/sub | solution.py:169
  181.7 38.9 %all-gather.5.cloned.1.call-done = bf16[2048,3,128]{0,2,1:T(8,128)(2,1)} async-done(((bf16[512,3,128]{0,2,1:T(8,128)(2,1)}), bf16[2048,3,128]{0,2,1:T(8,128)(2,1)}) %all-gather.5.cloned.1.call-update) | async-done | bytes 1572880 | tf_op jit(solution)/shard_map/all_gather | solution.py:201
  220.6 37.6 %all-gather.3.cloned.1.call-done = bf16[2048,3,128]{0,2,1:T(8,128)(2,1)} async-done(((bf16[512,3,128]{0,2,1:T(8,128)(2,1)}), bf16[2048,3,128]{0,2,1:T(8,128)(2,1)}) %all-gather.3.cloned.1.call-update) | async-done | bytes 1572880 | tf_op jit(solution)/shard_map/all_gather | solution.py:200
  260.3 72.4 %while.87 = (s32[]{:T(128)}, f32[3,8,512]{2,1,0:T(8,128)}, f32[3,8,512]{2,1,0:T(8,128)}, f32[3,8,512,16]{2,3,1,0:T(8,128)}, s32[512]{0:T(512)S(1)}, /*index=5*/b...) while((s32[]{:T(128)}, f32[3,8,512]{2,1,0:T(8,128)}, ...), condition=%wide.region_11.12_spmd, body=%wide.region_4.11_spmd.sunk | while | flops 161898512 | bytes 30925548 | solution.py:129
  261.6 32.7 %conditional.4 = (f32[3,8,512]{2,1,0:T(8,128)}, f32[3,8,512]{2,1,0:T(8,128)}, f32[3,8,512,16]{2,3,1,0:T(8,128)}) conditional(s32[]{:T(128)} %convert_element_type.330, (s32[]{:T(128)}, pred[]{:T(512)}, bf16[2048,3,128]{0,2,1:T(8,128)(2,1)}, bf16[2048,3,128]{0,2,1:T(8,128)(2,1)}, s32[512]{0:T(512)S(1)}, /*index=5*/f32[3,8,512]{2,1,0:T(8,128)}, ...), branch_computations={%region_5.9_spmd, %region_10.10_spmd} | conditional | flops 161898496 | bytes 29155664 | solution.py:107
  263.7 30.6 %while.85 = (s32[]{:T(128)}, f32[3,8,512]{2,1,0:T(8,128)}, f32[3,8,512]{2,1,0:T(8,128)}, f32[3,8,512,16]{2,3,1,0:T(8,128)}, f32[3,8,512]{2,1,0:T(8,128)}, /*inde...) while((s32[]{:T(128)}, f32[3,8,512]{2,1,0:T(8,128)}, ...), condition=%wide.region_9.8_spmd.clone, body=%wide.region_6.7_spmd.clone.sunk | while | flops 161890304 | bytes 27580584 | solution.py:82
  300.4 5.0 conditional.4
  311.6 5.0 conditional.4
  322.8 5.0 conditional.4
  338.6 8.2 multiply_convert_fusion.3
  367.1 70.0 %while.88 = (s32[]{:T(128)}, f32[3,8,512,16]{2,3,1,0:T(8,128)}, bf16[4,512,3,256]{1,3,2,0:T(8,128)(2,1)}, s32[4]{0:T(128)S(1)}, s32[512]{0:T(512)S(1)}, /*index=...) while((s32[]{:T(128)}, f32[3,8,512,16]{2,3,1,0:T(8,128)}, ...), condition=%wide.region_22.23_spmd, body=%wide.region_17.22_spmd.sunk | while | flops 358563840 | bytes 54789884 | solution.py:320
  372.9 42.9 %conditional.5 = (f32[3,8,512,16]{2,3,1,0:T(8,128)}, bf16[1,512,3,256]{1,3,2,0:T(8,128)(2,1)S(1)}) conditional(s32[]{:T(128)} %bitcast.301, (s32[]{:T(128)}, s32[1,512]{1,0:T(1,128)S(1)}, s32[]{:T(128)}, s32[512]{0:T(512)S(1)}, f32[3,8,512,16]{2,3,1,0:T(8,128)}, /*index=5*/bf16[3,8,512,16]{2,3,1,0:T(8,128)(2,1)S(1)}, ...), branch_computations={%region_18.20_spmd.clone, %region_21.21_spmd} | conditional | flops 358555648 | bytes 51639724 | solution.py:317
  372.9 39.6 %while.86 = (s32[]{:T(128)}, f32[3,8,512,16]{2,3,1,0:T(8,128)}, bf16[3,8,512,16]{2,3,1,0:T(8,128)(2,1)}, bf16[3,8,512,16]{2,3,1,0:T(8,128)(2,1)}, f32[3,8,512,16...) while((s32[]{:T(128)}, f32[3,8,512,16]{2,3,1,0:T(8,128)}, ...), condition=%wide.region_20.19_spmd.clone, body=%wide.region_19.18_spmd.clone.sunk | while | flops 356974592 | bytes 48489756 | solution.py:295
  391.1 4.5 multiply_convert_fusion.9
  437.1 4.7 copy.138
  441.9 4.7 copy.185
  453.6 6.0 reduce-scatter.16.cloned.1.call-done
  459.6 19.5 %reduce-scatter.18.cloned.1.call-done = bf16[32,512]{1,0:T(8,128)(2,1)} async-done(((bf16[128,512]{1,0:T(8,128)(2,1)}), bf16[32,512]{1,0:T(8,128)(2,1)}) %reduce-scatter.18.cloned.1.call-update) | async-done | bytes 32784 | tf_op jit(solution)/shard_map/reduce_scatter | solution.py:418
  479.1 19.6 %reduce-scatter.20.cloned.1.call-done = bf16[128,128]{1,0:T(8,128)(2,1)} async-done(((bf16[512,128]{1,0:T(8,128)(2,1)}), bf16[128,128]{1,0:T(8,128)(2,1)}) %reduce-scatter.20.cloned.1.call-update) | async-done | bytes 32784 | tf_op jit(solution)/shard_map/reduce_scatter | solution.py:421
  498.7 214.0 %reduce-scatter.10.cloned.1.call-done = bf16[512,3,256]{2,0,1:T(8,128)(2,1)} async-done(((bf16[2048,3,256]{2,0,1:T(8,128)(2,1)}), bf16[512,3,256]{2,0,1:T(8,128)(2,1)}) %reduce-scatter.10.cloned.1.call-update) | async-done | bytes 786448 | tf_op jit(solution)/shard_map/reduce_scatter | solution.py:324
  725.0 5.8 fusion.80
  734.3 4.6 copy.149
  739.1 7.8 multiply_convert_fusion.2
  753.3 4.6 copy.148
  758.0 5.5 fusion.134
  772.0 10.7 %all-reduce.4 = (bf16[16,128]{1,0:T(8,128)(2,1)S(1)}, bf16[128]{0:T(256)(128)(2,1)S(1)}, bf16[128]{0:T(256)(128)(2,1)S(1)}) all-reduce(bf16[16,128]{1,0:T(8,128)(2,1)S(1)} %copy.152, bf16[128]{0:T(256)(128)(2,1)} %get-tuple-element.850, bf16[128]{0:T(256)(128)(2,1)S(1)} %copy-done.46), channel_id=3, replica_groups=mesh['seq'=8,'blk'=4] {'blk'}, use_global_device_ids=true, to_apply=%region_27.28.clone | all-reduce | flops 2304 | bytes 9216
  782.8 5.9 reduce-scatter.22.cloned.1.call-done
  789.6 18.8 %reduce-scatter.14.cloned.1.call-done = bf16[32,384]{1,0:T(8,128)(2,1)} async-done(((bf16[128,384]{1,0:T(8,128)(2,1)}), bf16[32,384]{1,0:T(8,128)(2,1)}) %reduce-scatter.14.cloned.1.call-update) | async-done | bytes 24592 | tf_op jit(solution)/shard_map/reduce_scatter | solution.py:409
  808.4 27.5 %all-reduce.6 = (f32[4,128]{1,0:T(4,128)}, f32[32,256]{0,1:T(8,128)S(1)}, f32[32,128]{1,0:T(8,128)}, f32[32]{0:T(128)}, f32[32,384]{1,0:T(8,128)}, /*index=5*/f3...) all-reduce(f32[4,128]{1,0:T(4,128)S(1)} %dynamic-slice_convert_fusi, ...), channel_id=1, replica_groups=mesh['seq'=8,'blk'=4] {'seq'}, use_global_device_ids=true, to_apply=%region_28.29 | all-reduce | flops 62016 | bytes 373248 | tf_op jit(solution)/shard_map/psum | solution.py:425
  (321 shorter events, 223.3 us)
Async XLA Ops:
  7.2 213.4 %all-gather.5.cloned.1.call-start = ((), (), s32[]{:S(2)}) async-start(), calls=%async_computation.8 | async-start | bytes 1966080 | tf_op jit(solution)/shard_map/all_gather | solution.py:201
  9.1 16.5 %copy-start.31 = (bf16[16,8,16,1,1]{0,2,4,3,1:T(8,128)(2,1)}, bf16[16,8,16,1,1]{0,2,4,3,1:T(8,128)(2,1)S(1)}, u32[]{:S(2)}) copy-start(bf16[16,8,16,1,1]{0,2,4,3,1:T(8,128)(2,1)S(1)} %copy.170) | copy-start | bytes 12292
  162.5 5.3 copy-start.1
  163.3 6.1 copy-start.40
  171.7 8.9 %copy-start.34 = (f32[512,3]{0,1:T(4,128)}, f32[512,3]{0,1:T(4,128)S(1)}, u32[]{:S(2)}) copy-start(f32[512,3]{0,1:T(4,128)S(1)} %div.109) | copy-start | bytes 18436
  175.8 84.6 %copy-start.36 = (f32[512,3]{0,1:T(4,128)}, f32[512,3]{0,1:T(4,128)S(1)}, u32[]{:S(2)}) copy-start(f32[512,3]{0,1:T(4,128)S(1)} %rsqrt.20) | copy-start | bytes 18436
  180.6 77.5 %all-gather.3.cloned.1.call-start = ((), (), s32[]{:S(2)}) async-start(), calls=%async_computation.7 | async-start | bytes 1966080 | tf_op jit(solution)/shard_map/all_gather | solution.py:200
  181.4 278.2 %reduce-scatter.16.cloned.1.call-start = ((), (), s32[]{:S(2)}) async-start(), calls=%async_computation.12 | async-start | bytes 40960 | tf_op jit(solution)/shard_map/reduce_scatter | solution.py:412
  336.5 11.9 %copy-start.4 = (f32[512,3,128]{2,0,1:T(8,128)}, f32[512,3,128]{2,0,1:T(8,128)S(1)}, u32[]{:S(2)}) copy-start(f32[512,3,128]{2,0,1:T(8,128)S(1)} %get-tuple-element.980) | copy-start | bytes 2359300
  337.0 11.3 %copy-start.38 = (f32[512,3]{0,1:T(4,128)}, f32[512,3]{0,1:T(4,128)S(1)}, u32[]{:S(2)}) copy-start(f32[512,3]{0,1:T(4,128)S(1)} %add_rsqrt_fusion.1) | copy-start | bytes 18436
  338.6 8.3 copy-start.27
  338.6 8.3 copy-start.42
  351.1 6.6 copy-start.22
  358.6 120.5 %reduce-scatter.18.cloned.1.call-start = ((), (), s32[]{:S(2)}) async-start(), calls=%async_computation.13 | async-start | bytes 163840 | tf_op jit(solution)/shard_map/reduce_scatter | solution.py:418
  363.2 135.5 %reduce-scatter.20.cloned.1.call-start = ((), (), s32[]{:S(2)}) async-start(), calls=%async_computation.14 | async-start | bytes 163840 | tf_op jit(solution)/shard_map/reduce_scatter | solution.py:421
  366.1 346.7 %reduce-scatter.10.cloned.1.call-start = ((), (), s32[]{:S(2)}) async-start(), calls=%async_computation.9 | async-start | bytes 3932160 | tf_op jit(solution)/shard_map/reduce_scatter | solution.py:324
  441.8 341.0 %reduce-scatter.12.cloned.1.call-start = ((), (), s32[]{:S(2)}) async-start(), calls=%async_computation.10 | async-start | bytes 40960 | tf_op jit(solution)/shard_map/reduce_scatter | solution.py:403
  449.6 265.0 %copy-start.35 = (f32[512,3]{0,1:T(4,128)S(1)}, f32[512,3]{0,1:T(4,128)}, u32[]{:S(2)}) copy-start(f32[512,3]{0,1:T(4,128)} %copy-done.34) | copy-start | bytes 18436
  449.6 265.0 %copy-start.37 = (f32[512,3]{0,1:T(4,128)S(1)}, f32[512,3]{0,1:T(4,128)}, u32[]{:S(2)}) copy-start(f32[512,3]{0,1:T(4,128)} %copy-done.36) | copy-start | bytes 18436
  450.6 264.1 %copy-start.44 = (f32[128]{0:T(128)S(1)}, f32[128]{0:T(128)}, u32[]{:S(2)}) copy-start(f32[128]{0:T(128)} %param.30) | copy-start | bytes 1540
  712.7 6.2 copy-start.14
  722.1 66.7 %reduce-scatter.22.cloned.1.call-start = ((), (), s32[]{:S(2)}) async-start(), calls=%async_computation.15 | async-start | bytes 81920
  725.0 5.8 copy-start.2
  725.0 5.8 copy-start.3
  739.1 7.8 copy-start.32
  758.0 5.5 copy-start.8
  758.0 5.5 copy-start.9
  758.0 5.5 copy-start.33
  763.4 6.2 copy-start.25
  763.5 8.5 %copy-start.46 = (bf16[128]{0:T(256)(128)(2,1)S(1)}, bf16[128]{0:T(256)(128)(2,1)}, u32[]{:S(2)}) copy-start(bf16[128]{0:T(256)(128)(2,1)} %get-tuple-element.848) | copy-start | bytes 772
  763.5 44.9 %copy-start.43 = (bf16[32,128]{1,0:T(8,128)(2,1)S(1)}, bf16[32,128]{1,0:T(8,128)(2,1)}, u32[]{:S(2)}) copy-start(bf16[32,128]{1,0:T(8,128)(2,1)} %reduce-scatter.16.cloned.1.call-done) | copy-start | bytes 24580
  769.6 38.8 %reduce-scatter.14.cloned.1.call-start = ((), (), s32[]{:S(2)}) async-start(), calls=%async_computation.11 | async-start | bytes 122880 | tf_op jit(solution)/shard_map/reduce_scatter | solution.py:409
  (37 other events, 115.3 us)
Sparse Core Ops, SparseCore 0:
  180.7 39.7 all-gather.4
  222.1 35.9 all-gather.2
  358.7 100.8 reduce-scatter.15
  461.8 17.3 reduce-scatter.17
  481.2 17.4 reduce-scatter.19
  501.0 211.7 reduce-scatter.9
  722.2 18.9 reduce-scatter.11
  769.7 18.9 reduce-scatter.21
  791.1 17.2 reduce-scatter.13
where the time goes:
time: 856 us; the launch traced here: 843 us
  waiting for transfers between devices  361 us (42%)
  other arithmetic  175 us (20%)
  local copies, waits for them, and re-layouts  123 us (14%)
  matrix products  118 us (14%)
  blocking collectives  38.2 us (4%)
  between operations  16 us (2%)
  loops' own time  11.1 us (1%)
    reduce_scatter x1, waiting for transfers between devices, per_device(): lax.psum_scatter(term_all.astype(jnp.bfloat16), 'blk', scatter_dimension=...  214 us
    sub x1, other arithmetic, per_device(): stem_probs = jax.nn.softmax(stem_scores, axis=-1)  130 us
    all_gather x1, waiting for transfers between devices, per_device(): lax.all_gather(value_part, 'blk', axis=0, tiled=True)  38.9 us
    all_gather x1, waiting for transfers between devices, per_device(): lax.all_gather(key_part, 'blk', axis=0, tiled=True)  37.6 us
    psum x1, blocking collectives, per_device(): lax.psum((shares[0], shares[1], shares[2], shares[3], shares[4], shares[5...  27.5 us
    while x48, local copies, waits for them, and re-layouts  19.8 us
    reduce_scatter x1, waiting for transfers between devices, per_device(): lax.psum_scatter(local_grads[8].astype(jnp.bfloat16), 'blk', scatter_dime...  19.6 us
    reduce_scatter x1, waiting for transfers between devices, per_device(): lax.psum_scatter(local_grads[7].astype(jnp.bfloat16), 'blk', scatter_dime...  19.5 us
  transfers between devices with their start and end apart: 9, of which 8 were waited for; matrix products, arithmetic and copies ran while one was open for 16% of the time, Pallas kernels for 0%

commit v1 on v0

v1 whole, which is shorter than its diff:
```python
import functools
import math

import jax
import jax.numpy as jnp
from jax import lax
from jax.experimental import pallas as pl
from jax.experimental.pallas import tpu as pltpu
from jax.sharding import PartitionSpec as P

HEADS = 8
HEAD = 16
VIEWS = 3
GROUP = 8
EPSILON = 1e-05
FILL = -1e30
LOG2E = math.log2(math.e)
BF = jnp.bfloat16
F32 = jnp.float32
VMEM_BYTES = 58 * 2**20


def dot(left, right):
    return jnp.dot(left, right, preferred_element_type=F32)


def dot_nt(left, right):
    return lax.dot_general(left, right, (((1,), (1,)), ((), ())), preferred_element_type=F32)


def dot_tn(left, right):
    return lax.dot_general(left, right, (((0,), (0,)), ((), ())), preferred_element_type=F32)


def column_norm(values):
    center = values - jnp.mean(values, axis=0, keepdims=True)
    inverse = lax.rsqrt(jnp.mean(center * center, axis=0, keepdims=True) + EPSILON)
    return center * inverse, inverse


def column_norm_back(grad_unit, unit, inverse):
    centered = grad_unit - jnp.mean(grad_unit, axis=0, keepdims=True)
    return inverse * (centered - unit * jnp.mean(grad_unit * unit, axis=0, keepdims=True))


def stem_forward(s, x_ref, bias_ref, w1, block_mask, gather, wso_t, wqkv_t, gain, v_ref, p_ref, mix_ref, res_ref, n1_ref, send):
    steps, seqs = x_ref.shape[0], x_ref.shape[1]
    keys = x_ref.shape[2]
    view = keys // (VIEWS + 1)

    def group_body(g, carry):
        parts = []
        for k in range(GROUP):
            t = g * GROUP + k
            both = dot(x_ref[t, s], w1[...])
            values = both[:, :128].astype(BF)
            v_ref[s, t] = values
            rows = [
                both[view * i : view * (i + 1), 128:] + bias_ref[(i * steps + t) * seqs + s]
                for i in range(VIEWS)
            ]
            scores = jnp.concatenate(rows + [both[view * VIEWS :, 128:]], axis=0)
            top = jnp.max(scores, axis=0, keepdims=True)
            weights = jnp.exp2(scores - top)
            total = jnp.sum(weights, axis=0, keepdims=True)
            probs = (weights * (1.0 / total)).astype(BF)
            p_ref[s, t] = probs
            parts.append((dot_tn(values, probs) * block_mask[...]).astype(BF))
        mixed = dot(jnp.concatenate(parts, axis=1), gather[...])
        mix_ref[s, :, pl.ds(pl.multiple_of(g * 128, 128), 128)] = mixed.astype(BF)
        return carry

    lax.fori_loop(0, steps // GROUP, group_body, 0)
    residual = dot(wso_t[...], mix_ref[s])
    res_ref[s] = residual
    unit, _ = column_norm(residual)
    normed = (unit * gain[...]).astype(BF)
    n1_ref[s] = normed
    projected = dot(wqkv_t[...], normed)
    rows = projected.shape[0] // send.shape[0]
    per = rows // 3
    for j in range(send.shape[0]):
        part = projected[j * rows : (j + 1) * rows]
        send[j, s, 0:per, :] = (part[:per] * (LOG2E / math.sqrt(HEAD))).astype(BF)
        send[j, s, per:, :] = part[per:].astype(BF)


def attend_forward(s, att, onehot, mask_rows, ka_ref, o_ref, ob_ref, l_ref):
    tokens = att.shape[2]
    block = ob_ref.shape[3]
    zeros16 = jnp.zeros((16, block), BF)
    zeros32 = jnp.zeros((32, block), BF)
    stacked = jnp.concatenate(
        [att[s, 32:64, :], onehot[...], jnp.zeros((64, tokens), BF)], axis=0
    )
    ka_ref[...] = stacked.T

    def first(a, i):
        query = att[s, 16 * a : 16 * a + 16, block * i : block * (i + 1)]
        query = [query, zeros16] if a == 0 else [zeros16, query]
        tail = jnp.zeros((64, block), BF)
        scores = []
        if i:
            plain = jnp.concatenate(query + [zeros32, tail], axis=0)
            scores.append(dot(ka_ref[0 : block * i, :], plain))
        masked = jnp.concatenate(query + [mask_rows[...], tail], axis=0)
        scores.append(dot(ka_ref[block * i : block * (i + 1), :], masked))
        top = functools.reduce(jnp.maximum, [jnp.max(x, axis=0, keepdims=True) for x in scores])
        return scores, top

    def second(a, i, scores, top):
        start, out, total = 0, 0.0, 0.0
        for piece in scores:
            for c in range(0, piece.shape[0], block):
                weights = jnp.exp2(piece[c : c + block] - top)
                total = total + jnp.sum(weights, axis=0, keepdims=True)
                values = att[s, 64 + 16 * a : 80 + 16 * a, start : start + block]
                out = out + dot(values, weights.astype(BF))
                start += block
        out = out * (1.0 / total)
        o_ref[s, 16 * a : 16 * a + 16, block * i : block * (i + 1)] = out
        ob_ref[i, s, 16 * a : 16 * a + 16, :] = out.astype(BF)
        l_ref[s, a : a + 1, block * i : block * (i + 1)] = top + jnp.log2(total)

    units = [(a, i) for i in range(tokens // block) for a in range(2)]
    held = None
    for unit in units:
        now = first(*unit)
        if held is not None:
            second(*held[0], *held[1])
        held = (unit, now)
    second(*held[0], *held[1])


def feed_forward(s, orecv, res_ref, cot_ref, w, gain_row, out_ref, ga_ref, send, g_up, g_down, g_ao, g_gain):
    attended = jnp.concatenate([orecv[j, s] for j in range(orecv.shape[0])], axis=0)
    after = res_ref[s] + dot(w["ao_t"][...], attended)
    unit, inverse = column_norm(after)
    normed = (unit * gain_row[...]).astype(BF)
    pre = dot(w["up_t"][...], normed)
    cdf = 0.5 + 0.5 * lax.erf(pre * (1.0 / math.sqrt(2.0)))
    hidden = (pre * cdf).astype(BF)
    slope = cdf + pre * (jnp.exp2(pre * pre * (-0.5 * LOG2E)) * (1.0 / math.sqrt(2.0 * math.pi)))
    out_ref[s] = (after + dot(w["down_t"][...], hidden)).astype(BF)
    cot = cot_ref[s]
    g_down[...] += dot_nt(hidden, cot)
    grad_pre = (dot(w["down"][...], cot) * slope).astype(BF)
    g_up[...] += dot_nt(normed, grad_pre)
    grad_normed = dot(w["up"][...], grad_pre)
    g_gain[...] += grad_normed * unit
    grad_after = cot.astype(F32) + column_norm_back(grad_normed * gain_row[...], unit, inverse)
    ga_ref[s] = grad_after
    low = grad_after.astype(BF)
    g_ao[...] += dot_nt(attended, low)
    grad_att = dot(w["ao"][...], low).astype(BF)
    rows = grad_att.shape[0] // send.shape[0]
    for j in range(send.shape[0]):
        send[j, s] = grad_att[j * rows : (j + 1) * rows]


def three_parts(row):
    first = row.astype(BF).astype(F32)
    second = (row - first).astype(BF).astype(F32)
    return [first, second, row - first - second]


def attend_backward(s, att, dob, o_ref, l_ref, onehot, qa_ref, kb_ref, kd_ref, vb_ref, dq_ref, dk_ref, dv_ref, send):
    tokens = att.shape[2]
    block = send.shape[3]
    count = tokens // block
    rows = []
    dots = []
    for a in range(2):
        head = slice(16 * a, 16 * a + 16)
        rows += three_parts(-l_ref[s, a : a + 1, :])
        product = dob[s, head, :].astype(F32) * o_ref[s, head, :]
        down = -jnp.sum(product, axis=0, keepdims=True)
        high = down.astype(BF).astype(F32)
        dots += [high, down - high]
    small = jnp.concatenate(rows + dots + [jnp.zeros((6, tokens), F32)], axis=0).astype(BF)
    stacked = jnp.concatenate(
        [att[s, 0:32, :], dob[s], small, onehot[...], jnp.zeros((16, tokens), BF)], axis=0
    )
    qa_ref[...] = stacked.T
    for a in range(2):
        keys = att[s, 32 + 16 * a : 48 + 16 * a, :]
        kb_ref[a, 16 * a : 16 * a + 16, :] = keys
        kd_ref[a, 16 * a : 16 * a + 16, :] = keys
        vb_ref[a, 32 + 16 * a : 48 + 16 * a, :] = att[s, 64 + 16 * a : 80 + 16 * a, :]

    def span(i):
        return slice(block * i, block * (i + 1))

    def first(a, i, j):
        left = qa_ref[span(i), :]
        keys = kd_ref if i == j else kb_ref
        return dot(left, keys[a, :, span(j)]), dot(left, vb_ref[a, :, span(j)])

    def second(a, i, j, scores, grads):
        probs = jnp.exp2(scores)
        low = probs.astype(BF)
        grad = (probs * grads).astype(BF)
        head = slice(16 * a, 16 * a + 16)
        add_v = dot(dob[s, head, span(i)], low)
        add_k = dot(att[s, head, span(i)], grad)
        add_q = dot_nt(att[s, 32 + 16 * a : 48 + 16 * a, span(j)], grad)
        if i == j:
            dv_ref[head, span(j)] = add_v
            dk_ref[head, span(j)] = add_k
        else:
            dv_ref[head, span(j)] += add_v
            dk_ref[head, span(j)] += add_k
        if j == 0:
            dq_ref[head, span(i)] = add_q
        else:
            dq_ref[head, span(i)] += add_q

    units = [(a, i, j) for j in range(count) for i in range(j, count) for a in range(2)]
    held = None
    for unit in units:
        now = first(*unit)
        if held is not None:
            second(*held[0], *held[1])
        held = (unit, now)
    second(*held[0], *held[1])
    for i in range(count):
        send[i, s, 0:32, :] = (dq_ref[:, span(i)] * 0.25).astype(BF)
        send[i, s, 32:64, :] = (dk_ref[:, span(i)] * math.log(2.0)).astype(BF)
        send[i, s, 64:96, :] = dv_ref[:, span(i)].astype(BF)


def attend_constants(ones_ref, mask_ref, kb_ref, kd_ref, vb_ref):
    kb_ref[...] = jnp.zeros_like(kb_ref)
    kd_ref[...] = jnp.zeros_like(kd_ref)
    vb_ref[...] = jnp.zeros_like(vb_ref)
    for a in range(2):
        kb_ref[a, 64:80, :] = ones_ref[a]
        kd_ref[a, 64:80, :] = ones_ref[a]
        kd_ref[a, 80:112, :] = mask_ref[...]
        vb_ref[a, 64:80, :] = ones_ref[2 + a]


def stem_backward(s, x_ref, v_ref, p_ref, mix_ref, res_ref, n1_ref, ga_ref, precv, block_mask, spread, w, gain, gin_ref, gm_ref, g_qkv, g_gain, g_so, g_kv):
    steps = x_ref.shape[0]
    grad_proj = jnp.concatenate([precv[j, s] for j in range(precv.shape[0])], axis=0)
    g_qkv[...] += dot_nt(n1_ref[s], grad_proj)
    grad_normed = dot(w["qkv"][...], grad_proj)
    unit, inverse = column_norm(res_ref[s])
    g_gain[...] += grad_normed * unit
    grad_res = ga_ref[s] + column_norm_back(grad_normed * gain[...], unit, inverse)
    low = grad_res.astype(BF)
    g_so[...] += dot_nt(mix_ref[s], low)
    gm_ref[...] = dot(w["so"][...], low).astype(BF)

    def group_body(g, carry):
        wide = dot(gm_ref[:, pl.ds(pl.multiple_of(g * 128, 128), 128)], spread[...])
        total = jnp.zeros((128, 256), F32)
        for k in range(GROUP):
            t = g * GROUP + k
            grad_mixed = (wide[:, 128 * k : 128 * (k + 1)] * block_mask[...]).astype(BF)
            probs = p_ref[s, t]
            grad_probs = dot(v_ref[s, t], grad_mixed)
            weighted = probs.astype(F32) * grad_probs
            down = jnp.sum(weighted, axis=0, keepdims=True)
            grad_scores = (weighted - probs.astype(F32) * down).astype(BF)
            grad_values = dot_nt(probs, grad_mixed).astype(BF)
            both = jnp.concatenate([grad_values, grad_scores], axis=1)
            gin_ref[t, s] = dot(both, w["in"][...])
            total = total + dot_tn(x_ref[t, s], both)
        g_kv[...] += total
        return carry

    lax.fori_loop(0, steps // GROUP, group_body, 0)


def params():
    return pltpu.CompilerParams(vmem_limit_bytes=VMEM_BYTES)


def shape(dims, dtype):
    return jax.ShapeDtypeStruct(dims, dtype)


def per_device(
    stem_tokens, view_code, cotangent, stem_queries, w_stem_kv, w_stem_out,
    gain_one, w_qkv, w_attn_out, gain_two, w_up, w_down, nblk,
):
    steps, seqs, keys, width = stem_tokens.shape
    queries = stem_queries.shape[0]
    own = steps * queries
    tokens = own * nblk
    ff = w_up.shape[1]
    scale = 1.0 / math.sqrt(HEAD)
    lane = jnp.arange(128)
    block_mask = (lane[:, None] // HEAD == lane[None, :] // queries).astype(F32)
    row = jnp.arange(GROUP * 128)
    gather = ((row[:, None] // 128 == lane[None, :] // queries) & (row[:, None] % queries == lane[None, :] % queries)).astype(BF)
    spread = gather.T
    position = jnp.arange(tokens)
    onehot = ((position[None, :] // queries) % 32 == jnp.arange(32)[:, None]).astype(BF)
    local = jnp.arange(512) // queries
    mask_rows = jnp.where(jnp.arange(32)[:, None] > local[None, :], FILL, 0.0).astype(BF)
    mask_cols = jnp.where((position[None, :] // queries) % 32 > jnp.arange(32)[:, None], FILL, 0.0).astype(BF)
    patterns = [[0, 1, 2], [3, 4, 5], [6, 7], [8, 9]]
    ones_rows = jnp.stack([jnp.broadcast_to(sum((jnp.arange(16) == r) for r in rows)[:, None], (16, tokens)) for rows in patterns]).astype(BF)
    query_blocks = jnp.where(lane[:, None] // queries == lane[None, :] // HEAD, jnp.tile(stem_queries.astype(F32), (HEADS, 1)), 0.0)
    w_keys = w_stem_kv[:, :width].astype(F32)
    fold = jnp.dot(w_keys, query_blocks.T, precision=lax.Precision.HIGHEST) * scale
    w1 = jnp.concatenate([w_stem_kv[:, width:], (fold * LOG2E).astype(BF)], axis=1)
    w_in = jnp.concatenate([w_stem_kv[:, width:].T, fold.T.astype(BF)], axis=0)
    per = HEADS // nblk * HEAD
    order = w_qkv.reshape(width, 3, nblk, per).transpose(0, 2, 1, 3)
    wqkv = order.reshape(width, 3 * width)
    wqkv_t = wqkv.T
    present = jnp.stack([(view_code >> i) % 2 for i in range(VIEWS)])
    bias = jnp.where(present == 1, 0.0, FILL).astype(F32).reshape(-1)
    cot = cotangent.transpose(1, 2, 0)
    g1, g2 = gain_one[:, None], gain_two[:, None]
    vm = pl.BlockSpec(memory_space=pltpu.VMEM)
    sm = pl.BlockSpec(memory_space=pltpu.SMEM)

    def k_stem(x, b, w1_, bm, ga, so, qk, g, v, p, mix, res, n1, send):
        for s in range(seqs):
            stem_forward(s, x, b, w1_, bm, ga, so, qk, g, v, p, mix, res, n1, send)

    v_all, p_all, mix, res, n1, qkv_send = pl.pallas_call(
        k_stem,
        out_shape=[
            shape((seqs, steps, keys, 128), BF), shape((seqs, steps, keys, 128), BF), shape((seqs, 128, own), BF),
            shape((seqs, 128, own), F32), shape((seqs, 128, own), BF), shape((nblk, seqs, 3 * per, own), BF),
        ],
        in_specs=[vm, sm] + [vm] * 6, out_specs=[vm] * 6, compiler_params=params(),
    )(stem_tokens, bias, w1, block_mask, gather, w_stem_out.T, wqkv_t, g1)
    qkv = lax.all_to_all(qkv_send, "blk", 0, 0, tiled=True)
    att = qkv.transpose(1, 2, 0, 3).reshape(seqs, 3 * per, tokens)

    def k_att(att_, oh, mr, o, ob, l, ka):
        for s in range(seqs):
            attend_forward(s, att_, oh, mr, ka, o, ob, l)

    o_all, o_send, l_all = pl.pallas_call(
        k_att,
        out_shape=[shape((seqs, per, tokens), F32), shape((nblk, seqs, per, own), BF), shape((seqs, 8, tokens), F32)],
        in_specs=[vm] * 3, out_specs=[vm] * 3,
        scratch_shapes=[pltpu.VMEM((tokens, 128), BF)], compiler_params=params(),
    )(att, onehot, mask_rows)
    o_recv = lax.all_to_all(o_send, "blk", 0, 0, tiled=True)

    def k_ffn(orecv, res_, cot_, ao_t, up_t, down_t, ao, up, down, g, out, ga, send, g_up, g_down, g_ao, g_gain):
        w = {"ao_t": ao_t, "up_t": up_t, "down_t": down_t, "ao": ao, "up": up, "down": down}
        for ref in (g_up, g_down, g_ao, g_gain):
            ref[...] = jnp.zeros_like(ref)
        for s in range(seqs):
            feed_forward(s, orecv, res_, cot_, w, g, out, ga, send, g_up, g_down, g_ao, g_gain)

    out, ga, do_send, g_up, g_down, g_ao, g_gain2 = pl.pallas_call(
        k_ffn,
        out_shape=[
            shape((seqs, 128, own), BF), shape((seqs, 128, own), F32), shape((nblk, seqs, per, own), BF),
            shape((128, ff), F32), shape((ff, 128), F32), shape((128, 128), F32), shape((128, own), F32),
        ],
        in_specs=[vm] * 10, out_specs=[vm] * 7, compiler_params=params(),
    )(o_recv, res, cot, w_attn_out.T, w_up.T, w_down.T, w_attn_out, w_up, w_down, g2)
    do = lax.all_to_all(do_send, "blk", 0, 0, tiled=True).transpose(1, 2, 0, 3).reshape(seqs, per, tokens)

    def k_back(att_, do_, o, l, oh, on, mc, send, qa, kb, kd, vb, dq, dk, dv):
        attend_constants(on, mc, kb, kd, vb)
        for s in range(seqs):
            attend_backward(s, att_, do_, o, l, oh, qa, kb, kd, vb, dq, dk, dv, send)

    dp_send = pl.pallas_call(
        k_back,
        out_shape=shape((nblk, seqs, 3 * per, own), BF),
        in_specs=[vm] * 7, out_specs=vm,
        scratch_shapes=[pltpu.VMEM((tokens, 128), BF)] + [pltpu.VMEM((2, 128, tokens), BF)] * 3 + [pltpu.VMEM((per, tokens), F32)] * 3,
        compiler_params=params(),
    )(att, do, o_all, l_all, onehot, ones_rows, mask_cols)
    dp_recv = lax.all_to_all(dp_send, "blk", 0, 0, tiled=True)

    def k_stemb(x, v, p, mx, rs, n, ga_, pr, bm, sp, wq, wso, win, g, gin, g_qkv, g_gain, g_so, g_kv, gm):
        w = {"qkv": wq, "so": wso, "in": win}
        for ref in (g_qkv, g_gain, g_so, g_kv):
            ref[...] = jnp.zeros_like(ref)
        for s in range(seqs):
            stem_backward(s, x, v, p, mx, rs, n, ga_, pr, bm, sp, w, g, gin, gm, g_qkv, g_gain, g_so, g_kv)

    gin, g_qkv, g_gain1, g_so, g_kv = pl.pallas_call(
        k_stemb,
        out_shape=[
            shape((steps, seqs, keys, 128), F32), shape((128, 3 * width), F32), shape((128, own), F32),
            shape((128, 128), F32), shape((128, 256), F32),
        ],
        in_specs=[vm] * 14, out_specs=[vm] * 5,
        scratch_shapes=[pltpu.VMEM((128, own), BF)], compiler_params=params(),
    )(stem_tokens, v_all, p_all, mix, res, n1, ga, dp_recv, block_mask, spread, wqkv, w_stem_out, w_in, g1)

    g_value, g_fold = g_kv[:, :128], g_kv[:, 128:] * scale
    g_keys = jnp.dot(g_fold, query_blocks, precision=lax.Precision.HIGHEST)
    cross = jnp.dot(g_fold.T, w_keys, precision=lax.Precision.HIGHEST).reshape(HEADS, queries, HEADS, HEAD)
    g_queries = jnp.einsum("hnhe->nhe", cross).reshape(queries, width)
    g_qkv = g_qkv.reshape(width, nblk, 3, per).transpose(0, 2, 1, 3).reshape(width, 3 * width)
    grads = [
        g_queries, jnp.concatenate([g_keys, g_value], axis=1), g_so, jnp.sum(g_gain1, axis=1),
        g_qkv, g_ao, jnp.sum(g_gain2, axis=1), g_up, g_down,
    ]
    sizes = [g.size // nblk for g in grads]
    flat = jnp.concatenate([g.reshape(nblk, -1) for g in grads], axis=1)
    flat = lax.psum(flat, "seq")
    mine = lax.psum_scatter(flat, "blk", scatter_dimension=0, tiled=True).reshape(-1)
    results, at = [], 0
    for g, size in zip(grads, sizes):
        results.append(mine[at : at + size].reshape((g.shape[0] // nblk,) + g.shape[1:]))
        at += size
    return (out.transpose(2, 0, 1), gin, *results)


def solution(mesh):
    return jax.shard_map(
        functools.partial(per_device, nblk=mesh.shape["blk"]),
        mesh=mesh,
        in_specs=(P("blk", "seq"), P("blk", "seq"), P("blk", "seq")) + (P(),) * 9,
        out_specs=(P("blk", "seq"), P("blk", "seq")) + (P("blk"),) * 9,
        check_vma=False,
    )
```

time: 856 us -> 385 us (0.45)
  waiting for transfers between devices: 361 us -> 167 us
  other arithmetic: 175 us -> 8.78 us
  Pallas kernels: 0 us -> 126 us
  matrix products: 118 us -> 3.13 us
  local copies, waits for them, and re-layouts: 123 us -> 41.7 us
  blocking collectives: 38.2 us -> 0 us
  starting transfers between devices: 0.59 us -> 17.4 us
  loops' own time: 11.1 us -> 0 us
    reduce_scatter x6 -> x0, waiting for transfers between devices: 278 us -> none  [the longest x1 214 us: per_device(): lax.psum_scatter(term_all.astype(jnp.bfloat16), 'blk', scatter_dimension=...]
    sub x1 -> x0, other arithmetic: 130 us -> none  [per_device(): stem_probs = jax.nn.softmax(stem_scores, axis=-1)]
    pallas_call x0 -> x5, Pallas kernels: none -> 126 us  [the longest x1 36.7 us: per_device(): pl.pallas_call(k_back, out_shape=shape((nblk, seqs, 3 * per, own), BF), i...]
    dot_general x45 -> x3, matrix products: 118 us -> 3.13 us  [the longest x1 1.09 us: per_device(): jnp.dot(g_fold.T, w_keys, precision=lax.Precision.HIGHEST)]
    all_gather x2 -> x0, waiting for transfers between devices: 76.5 us -> none  [the longest x1 38.9 us: per_device(): lax.all_gather(value_part, 'blk', axis=0, tiled=True)]
    all_to_all x0 -> x4, waiting for transfers between devices: none -> 65.8 us  [the longest x1 27 us: per_device(): qkv = lax.all_to_all(qkv_send, 'blk', 0, 0, tiled=True)]
    psum x0 -> x1, waiting for transfers between devices: none -> 52.4 us  [per_device(): flat = lax.psum(flat, 'seq')]
    unnamed x10 -> x3, waiting for transfers between devices: 6.7 us -> 49.2 us
  transfers between devices with their start and end apart: 9 -> 6, of which waited for: 8 -> 6; matrix products, arithmetic and copies ran while one was open for 16% -> 3% of each run, Pallas kernels for 0% -> 0%
where the time goes in v1:
time: 385 us; the launch traced here: 380 us
  waiting for transfers between devices  167 us (43%)
  Pallas kernels  126 us (33%)
  local copies, waits for them, and re-layouts  41.7 us (11%)
  starting transfers between devices  17.4 us (5%)
  between operations  14.9 us (4%)
  other arithmetic  8.78 us (2%)
    psum x1, waiting for transfers between devices, per_device(): flat = lax.psum(flat, 'seq')  52.4 us
    unnamed x3, waiting for transfers between devices  49.2 us
    pallas_call x1, Pallas kernels, per_device(): pl.pallas_call(k_back, out_shape=shape((nblk, seqs, 3 * per, own), BF), i...  36.7 us
    pallas_call x1, Pallas kernels, per_device(): pl.pallas_call(k_stem, out_shape=[shape((seqs, steps, keys, 128), BF), sh...  31.4 us
    pallas_call x1, Pallas kernels, per_device(): pl.pallas_call(k_stemb, out_shape=[shape((steps, seqs, keys, 128), F32),...  31 us
    all_to_all x1, waiting for transfers between devices, per_device(): qkv = lax.all_to_all(qkv_send, 'blk', 0, 0, tiled=True)  27 us
    all_to_all x1, waiting for transfers between devices, per_device(): dp_recv = lax.all_to_all(dp_send, 'blk', 0, 0, tiled=True)  23.6 us
    pallas_call x1, Pallas kernels, per_device(): pl.pallas_call(k_att, out_shape=[shape((seqs, per, tokens), F32), shape((...  20.5 us
  transfers between devices with their start and end apart: 6, of which 6 were waited for; matrix products, arithmetic and copies ran while one was open for 3% of the time, Pallas kernels for 0%

profile of v1, /device:TPU:0, one launch (start us, length us, event | category | flops | bytes accessed | tf_op | source)
XLA Modules:
  0.0 379.7 jit_solution(9612100292727526100)
XLA Ops:
  8.6 1.5 copy.62
  12.6 1.4 copy.66.g
  15.7 1.0 copy.63
  17.4 1.0 and_convert_fusion.1.ga
  18.4 31.4 %shard_map.203 = (bf16[3,32,128,128]{3,2,1,0:T(8,128)(2,1)}, bf16[3,32,128,128]{3,2,1,0:T(8,128)(2,1)}, bf16[3,128,512]{2,1,0:T(8,128)(2,1)}, f32[3,128,512]{2,1...) custom-call(bf16[32,3,128,128]{3,2,1,0:T(8,128)(2,1)} %x.3, f32[288]{0:T(512)} %select_n.150.b, ...), custom_call_target="tpu_custom_call" | custom-call | tf_op jit(solution)/shard_map/pallas_call | solution.py:326
  49.9 6.5 %all-to-all-start = ((bf16[4,3,96,512]{3,2,1,0:T(8,128)(2,1)}), bf16[4,3,96,512]{3,2,1,0:T(8,128)(2,1)S(1)}, u32[]{:S(2)}, u32[]{:S(2)}) async-start(bf16[4,3,96,512]{3,2,1,0:T(8,128)(2,1)} %get-tuple-element.32), calls=%async_computation | async-start | bytes 2359296 | tf_op jit(solution)/shard_map/all_to_all | solution.py:334
  57.7 27.0 %all-to-all-done = bf16[4,3,96,512]{3,2,1,0:T(8,128)(2,1)S(1)} async-done(((bf16[4,3,96,512]{3,2,1,0:T(8,128)(2,1)}), bf16[4,3,96,512]{3,2,1,0:T(8,128)(2,1)S(1)}, u32[]{:S(2)}, u32[]{:S(2)}) %all-to-all-start) | async-done | bytes 1179680 | tf_op jit(solution)/shard_map/all_to_all | solution.py:334
  84.7 1.2 copy.82
  85.9 20.5 %shard_map.204 = (f32[3,32,2048]{2,1,0:T(8,128)}, bf16[4,3,32,512]{3,2,1,0:T(8,128)(2,1)}, f32[3,8,2048]{2,1,0:T(8,128)}) custom-call(bf16[3,96,2048]{2,1,0:T(8,128)(2,1)} %bitcast.45, bf16[32,2048]{1,0:T(8,128)(2,1)} %fusion.oh, bf16[32,512]{1,0:T(8,128)(2,1)} %select_convert_fusion.1.mr), custom_call_target="tpu_custom_call" | custom-call | tf_op jit(solution)/shard_map/pallas_call | solution.py:341
  106.5 3.5 all-to-all-start.1
  113.9 7.2 %all-to-all-done.1.orecv = bf16[4,3,32,512]{3,2,1,0:T(8,128)(2,1)S(1)} async-done(((bf16[4,3,32,512]{3,2,1,0:T(8,128)(2,1)}), bf16[4,3,32,512]{3,2,1,0:T(8,128)(2,1)S(1)}, u32[]{:S(2)}, u32[]{:S(2)}) %all-to-all-start.1) | async-done | bytes 393248 | tf_op jit(solution)/shard_map/all_to_all | solution.py:347
  121.8 6.8 %shard_map.205 = (bf16[3,128,512]{2,1,0:T(8,128)(2,1)}, f32[3,128,512]{2,1,0:T(8,128)}, bf16[4,3,32,512]{3,2,1,0:T(8,128)(2,1)}, f32[128,512]{1,0:T(8,128)}, f32...) custom-call(bf16[4,3,32,512]{3,2,1,0:T(8,128)(2,1)} %copy-done.1, ...), custom_call_target="tpu_custom_call" | custom-call | tf_op jit(solution)/shard_map/pallas_call | solution.py:356
  128.6 3.6 all-to-all-start.2
  134.0 7.9 %all-to-all-done.2 = bf16[4,3,32,512]{3,2,1,0:T(8,128)(2,1)S(1)} async-done(((bf16[4,3,32,512]{3,2,1,0:T(8,128)(2,1)}), bf16[4,3,32,512]{3,2,1,0:T(8,128)(2,1)S(1)}, u32[]{:S(2)}, u32[]{:S(2)}) %all-to-all-start.2) | async-done | bytes 393248 | tf_op jit(solution)/shard_map/all_to_all | solution.py:364
  142.7 36.7 %shard_map.206 = bf16[4,3,96,512]{3,2,1,0:T(8,128)(2,1)} custom-call(bf16[3,96,2048]{2,1,0:T(8,128)(2,1)} %bitcast.46, bf16[3,32,2048]{2,1,0:T(8,128)(2,1)} %bitcast.49, f32[3,32,2048]{2,1,0:T(8,128)} %get-tuple-element.42.o, f32[3,8,2048]{2,1,0:T(8,128)} %get-tuple-element.43.l, bf16[32,2048]{1,0:T(8,128)(2,1)} %fusion.oh, ...), custom_call_target="tpu_custom_call" | custom-call | tf_op jit(solution)/shard_map/pallas_call | solution.py:371
  179.5 3.7 all-to-all-start.3
  186.0 23.6 %all-to-all-done.3.pr = bf16[4,3,96,512]{3,2,1,0:T(8,128)(2,1)S(1)} async-done(((bf16[4,3,96,512]{3,2,1,0:T(8,128)(2,1)}), bf16[4,3,96,512]{3,2,1,0:T(8,128)(2,1)S(1)}, u32[]{:S(2)}, u32[]{:S(2)}) %all-to-all-start.3) | async-done | bytes 1179680 | tf_op jit(solution)/shard_map/all_to_all | solution.py:378
  209.7 1.0 copy-done
  210.7 31.0 %shard_map.207 = (f32[32,3,128,128]{3,2,1,0:T(8,128)}, f32[128,384]{1,0:T(8,128)}, f32[128,512]{1,0:T(8,128)}, f32[128,128]{1,0:T(8,128)}, f32[128,256]{1,0:T(8,128)}) custom-call(bf16[32,3,128,128]{3,2,1,0:T(8,128)(2,1)} %x.3, bf16[3,32,128,128]{3,2,1,0:T(8,128)(2,1)} %get-tuple-element.36.v, bf16[3,32,128,128]{3,2,1,0:T(8,128)(2,1)} %get-tuple-element.37.p, ...), custom_call_target="tpu_custom_call" | custom-call | tf_op jit(solution)/shard_map/pallas_call | solution.py:387
  241.6 1.1 fusion.1
  243.6 1.1 fusion.2
  244.7 1.1 reduce_sum.28
  248.5 1.7 dynamic-update-slice.4
  251.4 2.4 dynamic-update-slice.7
  253.8 2.1 dynamic-update-slice.8
  257.5 49.2 %all-reduce.6.cloned.1.call-done = f32[4,62016]{1,0:T(4,128)} async-done(((f32[4,62016]{1,0:T(4,128)}), f32[4,62016]{1,0:T(4,128)}) %all-reduce.6.cloned.1.call-update) | async-done | bytes 992272
  306.7 2.8 constant_dynamic-slice_fusion
  310.4 52.4 %all-reduce.4.cloned.1.call-done = f32[1,62016]{1,0:T(1,128)} async-done(((f32[1,62016]{1,0:T(1,128)}), f32[1,62016]{1,0:T(1,128)}) %all-reduce.4.cloned.1.call-update) | async-done | bytes 248080 | tf_op jit(solution)/shard_map/psum | solution.py:408
  365.9 1.9 fusion.41
  368.5 1.3 slice_bitcast_fusion
  369.8 1.3 slice.68
  371.0 1.4 fusion.42
  (105 shorter events, 28.6 us)
Async XLA Ops:
  49.9 34.9 %all-to-all-start = ((bf16[4,3,96,512]{3,2,1,0:T(8,128)(2,1)}), bf16[4,3,96,512]{3,2,1,0:T(8,128)(2,1)S(1)}, u32[]{:S(2)}, u32[]{:S(2)}) async-start(bf16[4,3,96,512]{3,2,1,0:T(8,128)(2,1)} %get-tuple-element.32), calls=%async_computation | async-start | bytes 2359296 | tf_op jit(solution)/shard_map/all_to_all | solution.py:334
  85.9 24.0 %copy-start.13 = (bf16[128,128]{1,0:T(8,128)(2,1)S(1)}, bf16[128,128]{1,0:T(8,128)(2,1)}, u32[]{:S(2)}) copy-start(bf16[128,128]{1,0:T(8,128)(2,1)} %ao.1) | copy-start | bytes 98308
  85.9 24.7 %copy-start.15 = (f32[128]{0:T(128)S(1)}, f32[128]{0:T(128)}, u32[]{:S(2)}) copy-start(f32[128]{0:T(128)} %param.21) | copy-start | bytes 1540
  85.9 25.5 %copy-start.4 = (bf16[128,512]{1,0:T(8,128)(2,1)S(1)}, bf16[128,512]{1,0:T(8,128)(2,1)}, u32[]{:S(2)}) copy-start(bf16[128,512]{1,0:T(8,128)(2,1)} %up.1) | copy-start | bytes 393220
  85.9 26.2 %copy-start.5 = (bf16[512,128]{1,0:T(8,128)(2,1)S(1)}, bf16[512,128]{1,0:T(8,128)(2,1)}, u32[]{:S(2)}) copy-start(bf16[512,128]{1,0:T(8,128)(2,1)} %down.1) | copy-start | bytes 393220
  85.9 27.0 %copy-start.6 = (bf16[512,3,128]{2,0,1:T(8,128)(2,1)S(1)}, bf16[512,3,128]{2,0,1:T(8,128)(2,1)}, u32[]{:S(2)}) copy-start(bf16[512,3,128]{2,0,1:T(8,128)(2,1)} %param.14) | copy-start | bytes 1179652
  106.5 14.6 %all-to-all-start.1 = ((bf16[4,3,32,512]{3,2,1,0:T(8,128)(2,1)}), bf16[4,3,32,512]{3,2,1,0:T(8,128)(2,1)S(1)}, u32[]{:S(2)}, u32[]{:S(2)}) async-start(bf16[4,3,32,512]{3,2,1,0:T(8,128)(2,1)} %get-tuple-element.33), calls=%async_computation.1 | async-start | bytes 786432 | tf_op jit(solution)/shard_map/all_to_all | solution.py:347
  121.1 0.7 copy-start.1
  128.6 13.3 %all-to-all-start.2 = ((bf16[4,3,32,512]{3,2,1,0:T(8,128)(2,1)}), bf16[4,3,32,512]{3,2,1,0:T(8,128)(2,1)S(1)}, u32[]{:S(2)}, u32[]{:S(2)}) async-start(bf16[4,3,32,512]{3,2,1,0:T(8,128)(2,1)} %get-tuple-element.41), calls=%async_computation.2 | async-start | bytes 786432 | tf_op jit(solution)/shard_map/all_to_all | solution.py:364
  179.4 3.8 copy-start.3
  179.4 6.0 %copy-start.10 = (f32[128,512]{1,0:T(8,128)S(1)}, f32[128,512]{1,0:T(8,128)}, u32[]{:S(2)}) copy-start(f32[128,512]{1,0:T(8,128)} %get-tuple-element.50) | copy-start | bytes 786436
  179.4 6.2 %copy-start.14 = (f32[128,128]{1,0:T(8,128)S(1)}, f32[128,128]{1,0:T(8,128)}, u32[]{:S(2)}) copy-start(f32[128,128]{1,0:T(8,128)} %get-tuple-element.49) | copy-start | bytes 196612
  179.4 6.3 %copy-start.9 = (f32[128,512]{1,0:T(8,128)S(1)}, f32[128,512]{1,0:T(8,128)}, u32[]{:S(2)}) copy-start(f32[128,512]{1,0:T(8,128)} %get-tuple-element.51) | copy-start | bytes 786436
  179.5 30.2 %all-to-all-start.3 = ((bf16[4,3,96,512]{3,2,1,0:T(8,128)(2,1)}), bf16[4,3,96,512]{3,2,1,0:T(8,128)(2,1)S(1)}, u32[]{:S(2)}, u32[]{:S(2)}) async-start(bf16[4,3,96,512]{3,2,1,0:T(8,128)(2,1)} %shard_map.206), calls=%async_computation.3 | async-start | bytes 2359296 | tf_op jit(solution)/shard_map/all_to_all | solution.py:378
  183.1 2.8 copy-start.8
  183.1 123.5 %all-reduce.6.cloned.1.call-start = ((), (), s32[]{:S(2)}) async-start(), calls=%async_computation.5 | async-start | bytes 1986560
  209.7 1.0 copy-start
  210.7 32.9 %copy-start.12 = (bf16[128,256]{1,0:T(8,128)(2,1)S(1)}, bf16[128,256]{1,0:T(8,128)(2,1)}, u32[]{:S(2)}) copy-start(bf16[128,256]{1,0:T(8,128)(2,1)} %param.16) | copy-start | bytes 196612
  241.6 5.1 %copy-start.11 = (f32[128,384]{1,0:T(8,128)S(1)}, f32[128,384]{1,0:T(8,128)}, u32[]{:S(2)}) copy-start(f32[128,384]{1,0:T(8,128)} %get-tuple-element.48) | copy-start | bytes 589828
  250.1 6.8 %copy-start.16 = (u32[32]{0:T(128)S(1)}, u32[32]{0:T(128)}, u32[]{:S(2)}) copy-start(u32[32]{0:T(128)} %constant.170) | copy-start | bytes 388
  253.8 55.7 %copy-start.7 = (bf16[3,128,512]{2,1,0:T(8,128)(2,1)S(1)}, bf16[3,128,512]{2,1,0:T(8,128)(2,1)}, u32[]{:S(2)}) copy-start(bf16[3,128,512]{2,1,0:T(8,128)(2,1)} %get-tuple-element.35) | copy-start | bytes 1179652
  255.9 1.0 copy-start.2
  256.9 106.0 %all-reduce.4.cloned.1.call-start = ((), (), s32[]{:S(2)}) async-start(), calls=%async_computation.4 | async-start | bytes 496640 | tf_op jit(solution)/shard_map/psum | solution.py:408
Sparse Core Ops, SparseCore 0:
  257.0 49.6 all-reduce.5
  310.1 52.7 all-reduce.3
